TPU v7x, 32 devices: a whole 2x2x4 slice. The times are simulated.
32 devices in a mesh: section: 2 (over x), dp: 4 (over z), tensor: 4 (over y, core).
Axes of the slice: x: 2, y: 2, z: 4, core: 2. Of those that a mesh axis runs over, the one named last changes fastest.
Arguments:
- tokens_in: bfloat16 [2, 1024, 3072], P(None, ('dp', 'tensor')), parts along dimension 1, may hold values from -6 to 6
- norm_gains: float32 [2, 3072], P('section'), may hold values from 0.25 to 1.75
- w_gate: bfloat16 [2, 1, 3072, 1024], P('section', None, None, 'tensor'), may hold values from -0.109375 to 0.109375
- w_up: bfloat16 [2, 1, 3072, 1024], P('section', None, None, 'tensor'), may hold values from -0.109375 to 0.109375
- w_down: bfloat16 [2, 1, 1024, 3072], P('section', None, 'tensor'), may hold values from -0.1875 to 0.1875
- route_ids: int32 [2, 2, 1024, 2], P('section', None, 'dp'), parts along dimension 2, may hold values from 0 to 7, all different within a row; in each aligned block of 256 rows (0 to 255, 256 to 511, ..., all dimensions but the last counted through in order) at most 128 rows name the same one
- route_gates: float32 [2, 2, 1024, 2], P('section', None, 'dp'), parts along dimension 2, may hold values from 0.1 to 1
Outputs:
- layer_out: bfloat16 [2, 2, 1024, 3072], P('section', None, ('dp', 'tensor')), parts along dimension 2
There are 4 independent parts, one for each index of `dp`. A program takes and returns all parts, laid end to end along the dimension named above; an argument that names none is the same for every part. Nothing has to cross between parts.
Inputs may be any that keep to these rules, and one draw needn't show every extreme that they name: `route_ids`: each token names two different experts; in each micro-batch of 256 tokens of one layer no expert is named by more than 128 tokens, a bound that some block reaches.
All inputs are finite; a program needn't handle non-finite values.
Results may differ from a plain program's by a relative error of at most 0.0055.
Values may be sent and summed in bfloat16 or wider, within the bound.
A program may use at most 64 MiB of HBM per device.

v0:
```python
import jax
import jax.numpy as jnp
from jax import lax
from jax.sharding import PartitionSpec as P

CAP = 128


def shifted(block, axis, distance):
    devices = range(lax.axis_size(axis))
    route = [(i - distance, i) for i in devices if i - distance in devices]
    return lax.ppermute(block, axis, route)


def normalize(rows, gain_row):
    values = rows.astype(jnp.float32)
    scale = lax.rsqrt(jnp.mean(values * values, axis=-1, keepdims=True) + 1e-05)
    return (values * scale * gain_row).astype(jnp.bfloat16)


def expert_partial(whole_rows, gate_part, up_part, down_part, ids_now, gates_now):
    picked = ids_now == 0
    chosen = jnp.sum(picked.astype(jnp.int32), axis=-1)
    weight = jnp.sum(jnp.where(picked, gates_now, 0.0), axis=-1)
    slot = jnp.cumsum(chosen) - 1
    positions = lax.broadcasted_iota(jnp.int32, (CAP, whole_rows.shape[0]), 0)
    select = ((slot[None, :] == positions) & (chosen[None, :] > 0)).astype(jnp.bfloat16)
    block = jnp.dot(select, whole_rows, preferred_element_type=jnp.float32).astype(jnp.bfloat16)
    gate_val = jnp.dot(block, gate_part[0], preferred_element_type=jnp.float32)
    up_val = jnp.dot(block, up_part[0], preferred_element_type=jnp.float32)
    act = (jax.nn.silu(gate_val) * up_val).astype(jnp.bfloat16)
    result = jnp.dot(act, down_part[0], preferred_element_type=jnp.float32)
    back = jnp.take(result, jnp.clip(slot, 0, CAP - 1), axis=0)
    total = back * weight[:, None]
    return total


def body(tokens_in, norm_gains, w_gate, w_up, w_down, route_ids, route_gates):
    section_index = lax.axis_index("section")
    at_first = section_index == 0
    gain_row = norm_gains[0]
    gate_part = w_gate[0]
    up_part = w_up[0]
    down_part = w_down[0]
    micro_count = tokens_in.shape[0]
    outputs = []
    carried = jnp.zeros_like(tokens_in[0])
    for step in range(micro_count + 1):
        inputs_now = jnp.where(at_first, tokens_in[min(step, micro_count - 1)], carried)
        which = jnp.clip(step - section_index, 0, micro_count - 1)
        ids_now = lax.dynamic_index_in_dim(route_ids[0], which, 0, keepdims=False)
        gates_now = lax.dynamic_index_in_dim(route_gates[0], which, 0, keepdims=False)
        ids_now, gates_now = (ids_now, gates_now)
        normed = normalize(inputs_now, gain_row)
        whole_rows = lax.all_gather(normed, "tensor", axis=0, tiled=True)
        partial_value = expert_partial(
            whole_rows, gate_part, up_part, down_part, ids_now, gates_now
        )
        summed = lax.psum_scatter(
            partial_value.astype(jnp.bfloat16), "tensor", scatter_dimension=0, tiled=True
        ).astype(jnp.float32)
        mixed = (inputs_now.astype(jnp.float32) + summed).astype(jnp.bfloat16)
        outputs.append(mixed)
        if step < micro_count:
            carried = shifted(mixed, "section", 1)
    blocks = [jnp.where(at_first, outputs[m], outputs[m + 1]) for m in range(micro_count)]
    return jnp.stack(blocks)[None]


def solution(mesh):
    return jax.shard_map(
        body,
        mesh=mesh,
        in_specs=(
            P(None, ("dp", "tensor"), None),
            P("section", None),
            P("section", None, None, "tensor"),
            P("section", None, None, "tensor"),
            P("section", None, "tensor", None),
            P("section", None, "dp", None),
            P("section", None, "dp", None),
        ),
        out_specs=P("section", None, ("dp", "tensor"), None),
        check_vma=False,
    )
```

profile of v0, /device:TPU:27, one launch (start us, length us, event | category | flops | bytes accessed | tf_op | source)
XLA Modules:
  0.0 234.8 jit_solution(8227788503903833381)
XLA Ops:
  6.6 1.3 fusion.53
  7.9 1.9 fusion.55
  9.8 0.0 all-gather.4.cloned.1.call-update
  9.8 0.0 reduce-scatter.4.cloned.1.call-start
  9.9 0.6 convert_reduce_fusion
  10.5 0.3 reduce-window.25
  10.8 0.1 slice.29
  10.9 0.6 select_reduce_fusion
  11.5 0.1 slice_reduce_fusion.2
  11.6 0.1 compare_and_fusion.2
  11.8 19.2 %all-gather.4.cloned.1.call-done = bf16[256,3072]{1,0:T(8,128)(2,1)} async-done(((bf16[64,3072]{1,0:T(8,128)(2,1)}), bf16[256,3072]{1,0:T(8,128)(2,1)}) %all-gather.4.cloned.1.call-update) | async-done | bytes 1572880 | tf_op jit(solution)/shard_map/all_gather | solution.py:55
  31.0 1.8 convolution_convert_fusion.2
  32.8 0.9 copy-done.4
  33.7 0.4 fusion.19
  34.1 2.7 %fusion.7 = f32[128,3072]{1,0:T(8,128)S(1)} fusion(bf16[1,1,256,3072]{3,2,1,0:T(8,128)(2,1)S(1)} %copy-done, bf16[128,3072]{1,0:T(8,128)(2,1)} %copy-done.4, bf16[1,1,3072,256]{3,2,1,0:T(8,128)(2,1)} %param.12, f32[128,256]{1,0:T(8,128)S(1)} %fusion.19), kind=kOutput, calls=%fused_computation.16 | convolution fusion | flops 402849792 | bytes 5636096 | tf_op jit(solution)/shard_map/dot_general | solution.py:32
  36.8 3.3 %gather_fusion = f32[256,3072]{1,0:T(8,128)} fusion(f32[128,3072]{1,0:T(8,128)S(1)} %fusion.7, s32[1024]{0:T(1024)S(1)} %pad_clamp_fusion.2), kind=kCustom, calls=%fused_computation.clone | custom fusion | bytes 6292480 | tf_op jit(solution)/shard_map/jit(_take)/gather | solution.py:33
  40.1 3.5 %fusion.2 = bf16[256,3072]{1,0:T(8,128)(2,1)} fusion(f32[256,3072]{1,0:T(8,128)} %gather_fusion, f32[256]{0:T(256)S(1)} %get-tuple-element.7, pred[256]{0:T(512)(128)(4,1)S(1)} %get-tuple-element.22), kind=kLoop, calls=%fused_computation.11 | loop fusion | flops 2359296 | bytes 4719872 | tf_op jit(solution)/shard_map/convert_element_type | solution.py:60
  43.7 0.0 reduce-scatter.4.cloned.1.call-update
  43.7 0.0 all-gather.6.cloned.1.call-start
  43.8 27.9 %reduce-scatter.4.cloned.1.call-done = bf16[64,3072]{1,0:T(8,128)(2,1)} async-done(((bf16[256,3072]{1,0:T(8,128)(2,1)}), bf16[64,3072]{1,0:T(8,128)(2,1)}) %reduce-scatter.4.cloned.1.call-update) | async-done | bytes 393232 | tf_op jit(solution)/shard_map/reduce_scatter | solution.py:59
  71.6 1.1 fusion.56
  72.7 1.3 collective-permute-start
  74.0 10.6 %collective-permute-done = bf16[64,3072]{1,0:T(8,128)(2,1)S(1)} collective-permute-done((bf16[64,3072]{1,0:T(8,128)(2,1)S(1)}, bf16[64,3072]{1,0:T(8,128)(2,1)S(1)}, u32[]{:S(2)}, u32[]{:S(2)}) %collective-permute-start) | collective-permute-done | bytes 393248 | tf_op jit(solution)/shard_map/ppermute | solution.py:12
  84.6 0.2 fusion.45
  84.9 0.9 fusion.47
  85.8 0.0 reduce-scatter.6.cloned.1.call-start
  85.8 1.1 reduce-window.29
  86.9 0.6 slice.32
  87.5 1.2 reduce-window.36
  88.8 0.8 slice_reduce_fusion.1
  89.5 1.3 compare_and_fusion.1
  90.8 0.6 pad_clamp_fusion.1
  91.5 1.2 broadcast_compare_fusion.1
  92.7 14.3 %all-gather.6.cloned.1.call-done = bf16[256,3072]{1,0:T(8,128)(2,1)} async-done(((bf16[64,3072]{1,0:T(8,128)(2,1)}), bf16[256,3072]{1,0:T(8,128)(2,1)}) %all-gather.6.cloned.1.call-update) | async-done | bytes 1572880 | tf_op jit(solution)/shard_map/all_gather | solution.py:55
  107.0 1.8 convolution_convert_fusion.1
  108.8 0.9 copy-done.5
  109.7 1.0 fusion.17
  110.7 2.7 %fusion.5 = f32[128,3072]{1,0:T(8,128)S(1)} fusion(bf16[1,1,256,3072]{3,2,1,0:T(8,128)(2,1)S(1)} %copy-done, bf16[128,3072]{1,0:T(8,128)(2,1)} %copy-done.5, bf16[1,1,3072,256]{3,2,1,0:T(8,128)(2,1)} %param.12, f32[128,256]{1,0:T(8,128)} %fusion.17), kind=kOutput, calls=%fused_computation.14 | convolution fusion | flops 402849792 | bytes 5636096 | tf_op jit(solution)/shard_map/dot_general | solution.py:32
  113.3 3.5 %gather_fusion.1 = f32[256,3072]{1,0:T(8,128)} fusion(f32[128,3072]{1,0:T(8,128)S(1)} %fusion.5, s32[1024]{0:T(1024)} %pad_clamp_fusion.1), kind=kCustom, calls=%fused_computation.1.clone | custom fusion | bytes 6292480 | tf_op jit(solution)/shard_map/jit(_take)/gather | solution.py:33
  116.8 3.6 %fusion.1 = bf16[256,3072]{1,0:T(8,128)(2,1)} fusion(f32[256,3072]{1,0:T(8,128)} %gather_fusion.1, f32[256]{0:T(256)S(1)} %copy-done.20, pred[256]{0:T(512)(128)(4,1)} %get-tuple-element.18), kind=kLoop, calls=%fused_computation.9 | loop fusion | flops 2359296 | bytes 4719872 | tf_op jit(solution)/shard_map/convert_element_type | solution.py:60
  120.4 0.0 reduce-scatter.6.cloned.1.call-update
  120.4 0.0 all-gather.8.cloned.1.call-start
  120.5 27.9 %reduce-scatter.6.cloned.1.call-done = bf16[64,3072]{1,0:T(8,128)(2,1)} async-done(((bf16[256,3072]{1,0:T(8,128)(2,1)}), bf16[64,3072]{1,0:T(8,128)(2,1)}) %reduce-scatter.6.cloned.1.call-update) | async-done | bytes 393232 | tf_op jit(solution)/shard_map/reduce_scatter | solution.py:59
  148.4 1.9 select_bitcast_fusion
  150.3 1.4 collective-permute-start.1
  151.7 10.6 %collective-permute-done.1 = bf16[64,3072]{1,0:T(8,128)(2,1)S(1)} collective-permute-done((bf16[64,3072]{1,0:T(8,128)(2,1)S(1)}, bf16[64,3072]{1,0:T(8,128)(2,1)S(1)}, u32[]{:S(2)}, u32[]{:S(2)}) %collective-permute-start.1) | collective-permute-done | bytes 393248 | tf_op jit(solution)/shard_map/ppermute | solution.py:12
  162.3 0.2 fusion.49
  162.6 0.9 fusion.51
  163.5 0.2 reduce-scatter.8.cloned.1.call-start
  163.8 0.3 reduce-window.37
  164.1 0.1 slice.34
  164.2 0.1 slice_reduce_fusion
  164.3 0.1 compare_and_fusion
  164.4 0.5 broadcast_compare_fusion
  164.9 19.7 %all-gather.8.cloned.1.call-done = bf16[256,3072]{1,0:T(8,128)(2,1)} async-done(((bf16[64,3072]{1,0:T(8,128)(2,1)}), bf16[256,3072]{1,0:T(8,128)(2,1)}) %all-gather.8.cloned.1.call-update) | async-done | bytes 1572880 | tf_op jit(solution)/shard_map/all_gather | solution.py:55
  184.6 1.8 convolution_convert_fusion
  186.4 0.9 copy-done.6
  187.3 1.0 fusion.15
  188.3 2.7 %fusion.3 = f32[128,3072]{1,0:T(8,128)S(1)} fusion(bf16[1,1,256,3072]{3,2,1,0:T(8,128)(2,1)S(1)} %copy-done, bf16[128,3072]{1,0:T(8,128)(2,1)} %copy-done.6, bf16[1,1,3072,256]{3,2,1,0:T(8,128)(2,1)} %param.12, f32[128,256]{1,0:T(8,128)} %fusion.15), kind=kOutput, calls=%fused_computation.12 | convolution fusion | flops 402849792 | bytes 5636096 | tf_op jit(solution)/shard_map/dot_general | solution.py:32
  191.0 3.3 %gather_fusion.2 = f32[256,3072]{1,0:T(8,128)} fusion(f32[128,3072]{1,0:T(8,128)S(1)} %fusion.3, s32[1024]{0:T(1024)S(1)} %pad_clamp_fusion), kind=kCustom, calls=%fused_computation.2.clone | custom fusion | bytes 6292480 | tf_op jit(solution)/shard_map/jit(_take)/gather | solution.py:33
  194.3 3.5 %fusion = bf16[256,3072]{1,0:T(8,128)(2,1)} fusion(f32[256,3072]{1,0:T(8,128)} %gather_fusion.2, f32[256]{0:T(256)S(1)} %copy-done.19, pred[256]{0:T(512)(128)(4,1)S(1)} %get-tuple-element.14), kind=kLoop, calls=%fused_computation.7 | loop fusion | flops 2359296 | bytes 4719872 | tf_op jit(solution)/shard_map/convert_element_type | solution.py:60
  197.9 27.9 %reduce-scatter.8.cloned.1.call-done = bf16[64,3072]{1,0:T(8,128)(2,1)} async-done(((bf16[256,3072]{1,0:T(8,128)(2,1)}), bf16[64,3072]{1,0:T(8,128)(2,1)}) %reduce-scatter.8.cloned.1.call-update) | async-done | bytes 393232 | tf_op jit(solution)/shard_map/reduce_scatter | solution.py:59
  225.8 1.1 fusion.58
  227.0 0.9 maximum_bitcast_fusion
  (53 shorter events, 0.3 us)
Async XLA Ops:
  6.5 27.5 %copy-start = (bf16[1,1,256,3072]{3,2,1,0:T(8,128)(2,1)S(1)}, bf16[1,1,256,3072]{3,2,1,0:T(8,128)(2,1)}, u32[]{:S(2)}) copy-start(bf16[1,1,256,3072]{3,2,1,0:T(8,128)(2,1)} %param.13) | copy-start | bytes 4718596
  6.5 3.3 %copy-start.15 = (s32[1,2,256,2]{2,3,1,0:T(2,128)S(1)}, s32[1,2,256,2]{2,3,1,0:T(2,128)}, u32[]{:S(2)}) copy-start(s32[1,2,256,2]{2,3,1,0:T(2,128)} %param.14) | copy-start | bytes 12292
  6.5 4.4 %copy-start.16 = (f32[1,2,256,2]{2,3,1,0:T(2,128)S(1)}, f32[1,2,256,2]{2,3,1,0:T(2,128)}, u32[]{:S(2)}) copy-start(f32[1,2,256,2]{2,3,1,0:T(2,128)} %param.15) | copy-start | bytes 12292
  6.5 24.5 %all-gather.4.cloned.1.call-start = ((), (), s32[]{:S(2)}) async-start(), calls=%async_computation.3 | async-start | bytes 1966080 | tf_op jit(solution)/shard_map/all_gather | solution.py:55
  9.8 23.9 %copy-start.1 = (bf16[1,1,3072,256]{3,2,1,0:T(8,128)(2,1)S(1)}, bf16[1,1,3072,256]{3,2,1,0:T(8,128)(2,1)}, u32[]{:S(2)}) copy-start(bf16[1,1,3072,256]{3,2,1,0:T(8,128)(2,1)} %param.11) | copy-start | bytes 4718596
  9.8 61.8 %reduce-scatter.4.cloned.1.call-start = ((), (), s32[]{:S(2)}) async-start(), calls=%async_computation.4 | async-start | bytes 1966080 | tf_op jit(solution)/shard_map/reduce_scatter | solution.py:59
  32.8 0.9 copy-start.4
  43.7 27.9 %copy-start.7 = (bf16[2,64,3072]{2,1,0:T(8,128)(2,1)S(1)}, bf16[2,64,3072]{2,1,0:T(8,128)(2,1)}, u32[]{:S(2)}) copy-start(bf16[2,64,3072]{2,1,0:T(8,128)(2,1)} %param.9) | copy-start | bytes 2359300
  43.7 41.2 %copy-start.14 = (f32[1,3072]{1,0:T(1,128)S(1)}, f32[1,3072]{1,0:T(1,128)}, u32[]{:S(2)}) copy-start(f32[1,3072]{1,0:T(1,128)} %param.10) | copy-start | bytes 36868
  43.7 63.3 %all-gather.6.cloned.1.call-start = ((), (), s32[]{:S(2)}) async-start(), calls=%async_computation.5 | async-start | bytes 1966080 | tf_op jit(solution)/shard_map/all_gather | solution.py:55
  72.7 1.3 copy-start.12
  72.7 11.9 %collective-permute-start = (bf16[64,3072]{1,0:T(8,128)(2,1)S(1)}, bf16[64,3072]{1,0:T(8,128)(2,1)S(1)}, u32[]{:S(2)}, u32[]{:S(2)}) collective-permute-start(bf16[64,3072]{1,0:T(8,128)(2,1)S(1)} %fusion.56), channel_id=1, source_target_pairs={{0,16},{1,17},{2,18},{3,19},{4,20},{5,21},{6,22},{7,23},{8,24},{9,... | collective-permute-start | bytes 1179656 | tf_op jit(solution)/shard_map/ppermute | solution.py:12
  85.8 23.9 %copy-start.2 = (bf16[1,1,3072,256]{3,2,1,0:T(8,128)(2,1)S(1)}, bf16[1,1,3072,256]{3,2,1,0:T(8,128)(2,1)}, u32[]{:S(2)}) copy-start(bf16[1,1,3072,256]{3,2,1,0:T(8,128)(2,1)} %param.11) | copy-start | bytes 4718596
  85.8 62.6 %reduce-scatter.6.cloned.1.call-start = ((), (), s32[]{:S(2)}) async-start(), calls=%async_computation.6 | async-start | bytes 1966080 | tf_op jit(solution)/shard_map/reduce_scatter | solution.py:59
  86.9 1.8 copy-start.17
  108.8 0.9 copy-start.5
  113.3 3.5 %copy-start.20 = (f32[256]{0:T(256)S(1)}, f32[256]{0:T(256)}, u32[]{:S(2)}) copy-start(f32[256]{0:T(256)} %get-tuple-element.8) | copy-start | bytes 3076
  120.4 28.0 %copy-start.13 = (bf16[64,3072]{1,0:T(8,128)(2,1)S(1)}, bf16[64,3072]{1,0:T(8,128)(2,1)}, u32[]{:S(2)}) copy-start(bf16[64,3072]{1,0:T(8,128)(2,1)} %copy-done.12) | copy-start | bytes 1179652
  120.4 41.9 %copy-start.8 = (bf16[2,64,3072]{2,1,0:T(8,128)(2,1)S(1)}, bf16[2,64,3072]{2,1,0:T(8,128)(2,1)}, u32[]{:S(2)}) copy-start(bf16[2,64,3072]{2,1,0:T(8,128)(2,1)} %param.9) | copy-start | bytes 2359300
  120.4 64.2 %all-gather.8.cloned.1.call-start = ((), (), s32[]{:S(2)}) async-start(), calls=%async_computation.7 | async-start | bytes 1966080 | tf_op jit(solution)/shard_map/all_gather | solution.py:55
  150.3 12.3 %copy-start.10 = (bf16[64,3072]{1,0:T(8,128)(2,1)}, bf16[64,3072]{1,0:T(8,128)(2,1)S(1)}, u32[]{:S(2)}) copy-start(bf16[64,3072]{1,0:T(8,128)(2,1)S(1)} %get-tuple-element.13) | copy-start | bytes 1179652
  150.3 13.4 %copy-start.18 = (s32[256]{0:T(256)S(1)}, s32[256]{0:T(256)}, u32[]{:S(2)}) copy-start(s32[256]{0:T(256)} %get-tuple-element.9) | copy-start | bytes 3076
  150.3 12.0 %collective-permute-start.1 = (bf16[64,3072]{1,0:T(8,128)(2,1)S(1)}, bf16[64,3072]{1,0:T(8,128)(2,1)S(1)}, u32[]{:S(2)}, u32[]{:S(2)}) collective-permute-start(bf16[64,3072]{1,0:T(8,128)(2,1)S(1)} %get-tuple-element.13), channel_id=1, source_target_pairs={{0,16},{1,17},{2,18},{3,19},{4,20},{5,21},{6,22},{7,23},{8,24},{9,... | collective-permute-start | bytes 1179656 | tf_op jit(solution)/shard_map/ppermute | solution.py:12
  163.5 23.8 %copy-start.3 = (bf16[1,1,3072,256]{3,2,1,0:T(8,128)(2,1)S(1)}, bf16[1,1,3072,256]{3,2,1,0:T(8,128)(2,1)}, u32[]{:S(2)}) copy-start(bf16[1,1,3072,256]{3,2,1,0:T(8,128)(2,1)} %param.11) | copy-start | bytes 4718596
  163.5 62.3 %reduce-scatter.8.cloned.1.call-start = ((), (), s32[]{:S(2)}) async-start(), calls=%async_computation.8 | async-start | bytes 1966080 | tf_op jit(solution)/shard_map/reduce_scatter | solution.py:59
  186.4 0.9 copy-start.6
  191.0 3.4 %copy-start.19 = (f32[256]{0:T(256)S(1)}, f32[256]{0:T(256)}, u32[]{:S(2)}) copy-start(f32[256]{0:T(256)} %get-tuple-element.6) | copy-start | bytes 3076
  197.9 28.0 %copy-start.11 = (bf16[64,3072]{1,0:T(8,128)(2,1)S(1)}, bf16[64,3072]{1,0:T(8,128)(2,1)}, u32[]{:S(2)}) copy-start(bf16[64,3072]{1,0:T(8,128)(2,1)} %copy-done.10) | copy-start | bytes 1179652
  197.9 29.1 %copy-start.9 = (bf16[1,64,3072]{2,1,0:T(8,128)(2,1)S(1)}, bf16[1,64,3072]{2,1,0:T(8,128)(2,1)}, u32[]{:S(2)}) copy-start(bf16[1,64,3072]{2,1,0:T(8,128)(2,1)} %get-tuple-element.12) | copy-start | bytes 1179652
Sparse Core Ops, SparseCore 0:
  9.9 21.0 all-gather.3
  43.8 27.7 reduce-scatter.3
  85.9 21.0 all-gather.5
  120.5 27.7 reduce-scatter.5
  163.6 20.9 all-gather.7
  198.0 27.7 reduce-scatter.7
where the time goes:
time: 237 us; the launch traced here: 235 us
  waiting for transfers between devices  158 us (67%)
  other arithmetic  29.4 us (12%)
  matrix products  15.8 us (7%)
  local copies, waits for them, and re-layouts  14.6 us (6%)
  between operations  13.7 us (6%)
  starting transfers between devices  3.09 us (1%)
    reduce_scatter x3, waiting for transfers between devices, body(): lax.psum_scatter(partial_value.astype(jnp.bfloat16), 'tensor', scatter_di...  83.7 us
    all_gather x3, waiting for transfers between devices, body(): whole_rows = lax.all_gather(normed, 'tensor', axis=0, tiled=True)  53.2 us
    ppermute x2, waiting for transfers between devices, shifted(): return lax.ppermute(block, axis, route)  21.1 us
    convert_element_type x3, other arithmetic, body(): partial_value.astype(jnp.bfloat16)  10.7 us
    gather x3, local copies, waits for them, and re-layouts, expert_partial(): back = jnp.take(result, jnp.clip(slot, 0, CAP - 1), axis=0)  10.2 us
    dot_general x3, matrix products, expert_partial(): result = jnp.dot(act, down_part[0], preferred_element_type=jnp.float32)  8.02 us
    dot_general x3, matrix products, expert_partial(): jnp.dot(select, whole_rows, preferred_element_type=jnp.float32)  5.37 us
  transfers between devices with their start and end apart: 8, of which 8 were waited for; matrix products, arithmetic and copies ran while one was open for 4% of the time, Pallas kernels for 0%

commit v1 on v0

v1 whole, which is shorter than its diff:
```python
import functools

import jax
import jax.numpy as jnp
from jax import lax
from jax.experimental import pallas as pl
from jax.experimental.pallas import tpu as pltpu
from jax.sharding import PartitionSpec as P

CAP = 128
HALF = CAP // 2
MESH = pl.DeviceIdType.MESH
F32 = jnp.float32
BF16 = jnp.bfloat16


def dot_nt(a, b):
    return lax.dot_general(a, b, (((1,), (1,)), ((), ())), preferred_element_type=F32)


def kernel(
    n, micro, tok_ref, gain_ref, route_ref, wg_hbm, wu_hbm, wd_hbm, out_ref,
    rows, wg, wu, wd, peer_route, blocks, term, from_mate, chip_sum, from_chip, sums, own_rows, result,
    tok_sem, w_sem, out_sem, route_sems,
    g_send, g_recv, f_send, a_send, a_recv, b_send, b_recv, c_send, c_recv, d_send, d_recv, e_send, e_recv,
):
    chips = n // 2
    rpd = tok_ref.shape[1]
    width = tok_ref.shape[2]
    tok = n * rpd
    cols = width // chips
    sec = lax.axis_index("section")
    me = lax.axis_index("tensor")
    chip = me // 2
    core = me % 2
    mate = chip * 2 + (1 - core)
    other = 1 - sec
    sends = []

    def chip_at(step):
        return lax.rem(chip + step, chips)

    def remote(src, dst, send, recv, **where):
        return pltpu.make_async_remote_copy(
            src_ref=src, dst_ref=dst, send_sem=send, recv_sem=recv, device_id=where, device_id_type=MESH
        )

    def rows_of(index):
        return pl.ds(pl.multiple_of(index * rpd, rpd), rpd)

    my_half = pl.ds(pl.multiple_of(core * HALF, HALF), HALF)
    mate_half = pl.ds(pl.multiple_of((1 - core) * HALF, HALF), HALF)

    def own_copy(m):
        return pltpu.make_async_copy(tok_ref.at[m], rows.at[m, rows_of(me), :], tok_sem.at[m])

    def weight_copies():
        pairs = ((wg_hbm, wg), (wu_hbm, wu), (wd_hbm, wd))
        return [pltpu.make_async_copy(src, dst, w_sem.at[i]) for i, (src, dst) in enumerate(pairs)]

    for m in range(micro):
        own_copy(m).start()
    for copy in weight_copies():
        copy.start()

    barrier = pltpu.get_barrier_semaphore()
    for step in range(1, chips):
        pl.semaphore_signal(barrier, inc=1, device_id={"tensor": chip_at(step) * 2 + core}, device_id_type=MESH)
    pl.semaphore_signal(barrier, inc=1, device_id={"tensor": mate}, device_id_type=MESH)
    pl.semaphore_signal(barrier, inc=1, device_id={"section": other}, device_id_type=MESH)
    pl.semaphore_wait(barrier, chips + 1)

    def gather(m, owner, target, from_tokens, send):
        place = rows.at[m, rows_of(owner), :]
        return remote(tok_ref.at[m] if from_tokens else place, place, send, g_recv.at[m, owner], tensor=target)

    first = []

    def route_copy():
        return remote(route_ref, peer_route, route_sems.at[0], route_sems.at[1], section=other)

    route_copy().start()
    first.append(route_copy())
    for m in range(micro):
        for step in range(1, chips):
            copy = gather(m, me, chip_at(step) * 2 + core, True, g_send.at[m, step])
            copy.start()
            first.append(copy)
        copy = gather(m, me, mate, True, g_send.at[m, 0])
        copy.start()
        first.append(copy)

    def forward(m):
        for step in range(1, chips):
            owner = chip_at(step) * 2 + core
            copy = gather(m, owner, mate, False, f_send.at[m, step])
            copy.wait_recv()
            copy.start()
            sends.append(copy)

    def gathered(m):
        own_copy(m).wait()
        for step in range(chips):
            owner = chip_at(step) * 2 + (1 - core)
            gather(m, owner, mate, False, f_send.at[m, step]).wait_recv()

    tri = (
        lax.broadcasted_iota(jnp.int32, (tok, tok), 0) <= lax.broadcasted_iota(jnp.int32, (tok, tok), 1)
    ).astype(F32).astype(BF16)

    def selection(ref, m):
        chosen = ref[m : m + 1, :]
        counts = jnp.dot(jnp.broadcast_to(chosen, (16, tok)).astype(BF16), tri, preferred_element_type=F32)
        slot = (counts[0:1, :] - 1.0).astype(jnp.int32)
        hit = (slot == lax.broadcasted_iota(jnp.int32, (CAP, tok), 0)) & (chosen > 0.5)
        return jnp.where(hit, 1.0, 0.0)

    def mine(select):
        pick = lax.broadcasted_iota(jnp.int32, (rpd, tok), 1) == lax.broadcasted_iota(
            jnp.int32, (rpd, tok), 0
        ) + me * rpd
        return dot_nt(pick.astype(F32).astype(BF16), select).astype(BF16)

    def take(m, select):
        for k in range(chips):
            at = pl.ds(k * cols, cols)
            blocks[m, :, at] = jnp.dot(select, rows[m, :, at], preferred_element_type=F32)

    def experts(m, select):
        weight = jnp.sum(select * route_ref[micro + m : micro + m + 1, :], axis=1, keepdims=True)
        block = blocks[m]
        scale = lax.rsqrt(jnp.mean(block * block, axis=1, keepdims=True) + 1e-05)
        normed = (block * scale * gain_ref[...]).astype(BF16)
        gate = jnp.dot(normed, wg[...], preferred_element_type=F32)
        up = jnp.dot(normed, wu[...], preferred_element_type=F32)
        act = (gate / (1.0 + jnp.exp(-gate)) * up).astype(BF16)
        for k in range(chips):
            part = jnp.dot(act, wd[:, k * cols : (k + 1) * cols], preferred_element_type=F32)
            term[m, k] = (part * weight).astype(BF16)
        copy = to_mate(m)
        copy.start()
        sends.append(copy)

    def to_mate(m):
        return remote(term.at[m, :, mate_half, :], from_mate.at[m], a_send.at[m], a_recv.at[m], tensor=mate)

    def to_chip(m, step):
        there = chip_at(step)
        return remote(
            chip_sum.at[m, there], from_chip.at[m, step], b_send.at[m, step], b_recv.at[m, step],
            tensor=there * 2 + core,
        )

    def piece(layer, m, k, half):
        return sums.at[layer, m, k, half, :]

    def to_section(m):
        place = piece(0, m, chip, my_half)
        return remote(place, place, c_send.at[m], c_recv.at[m], section=other)

    def spread(layer, m, step):
        place = piece(layer, m, chip, my_half)
        return remote(
            place, place, d_send.at[layer, m, step], d_recv.at[layer, m, step], tensor=chip_at(step) * 2 + core
        )

    def share(layer, m, step, half):
        place = piece(layer, m, chip_at(step), half)
        return remote(place, place, e_send.at[layer, m, step], e_recv.at[layer, m, step], tensor=mate)

    def go(copy):
        copy.start()
        sends.append(copy)

    def reduce_core(m):
        to_mate(m).wait_recv()
        for k in range(chips):
            chip_sum[m, k] = (term[m, k, my_half, :].astype(F32) + from_mate[m, k].astype(F32)).astype(BF16)
        for step in range(1, chips):
            go(to_chip(m, step))

    def reduce_chip(layer, m):
        total = chip_sum[m, chip].astype(F32)
        for step in range(1, chips):
            to_chip(m, step).wait_recv()
            total = total + from_chip[m, step].astype(F32)
        sums[layer, m, chip, my_half, :] = total.astype(BF16)

    def start_spread(layer, m):
        for step in range(1, chips):
            go(spread(layer, m, step))
        go(share(layer, m, 0, my_half))

    def finish_spread(layer, m):
        for step in range(1, chips):
            spread(layer, m, step).wait_recv()
        for step in range(1, chips):
            go(share(layer, m, step, my_half))

    def spread_done(layer, m):
        for step in range(chips):
            share(layer, m, step, mate_half).wait_recv()

    def out_copy(m):
        return pltpu.make_async_copy(result.at[m], out_ref.at[m], out_sem.at[m])

    def add_own(layer, m, source, select_own, target):
        for k in range(chips):
            at = pl.ds(k * cols, cols)
            more = jnp.dot(select_own, sums[layer, m, k], preferred_element_type=F32)
            target[m, :, at] = (source[:, at].astype(F32) + more).astype(BF16)

    def wait_sends():
        for copy in sends:
            copy.wait_send()
        sends.clear()

    @pl.when(sec == 0)
    def _():
        selects = [selection(route_ref, m) for m in range(micro)]
        for copy in weight_copies():
            copy.wait()
        forward(0)
        gathered(0)
        take(0, selects[0].astype(BF16))
        experts(0, selects[0])
        forward(1)
        reduce_core(0)
        gathered(1)
        take(1, selects[1].astype(BF16))
        experts(1, selects[1])
        reduce_chip(0, 0)
        go(to_section(0))
        start_spread(0, 0)
        reduce_core(1)
        finish_spread(0, 0)
        reduce_chip(0, 1)
        go(to_section(1))
        start_spread(0, 1)
        for m in range(micro):
            if m == 1:
                finish_spread(0, 1)
            spread_done(0, m)
            add_own(0, m, rows.at[m, rows_of(me), :], mine(selects[m].astype(BF16)), result)
            out_copy(m).start()
        route_copy().wait_recv()
        wait_sends()
        for m in range(micro):
            out_copy(m).wait()

    @pl.when(sec == 1)
    def _():
        selects = [selection(route_ref, m) for m in range(micro)]
        for copy in weight_copies():
            copy.wait()
        route_copy().wait_recv()
        before = [selection(peer_route, m).astype(BF16) for m in range(micro)]
        for m in range(micro):
            forward(m)
            gathered(m)
            take(m, selects[m].astype(BF16))

        def second(m):
            spread_done(0, m)
            link = dot_nt(selects[m].astype(BF16), before[m]).astype(BF16)
            for k in range(chips):
                at = pl.ds(k * cols, cols)
                more = jnp.dot(link, sums[0, m, k], preferred_element_type=F32)
                blocks[m, :, at] = (blocks[m, :, at] + more).astype(BF16).astype(F32)
            experts(m, selects[m])
            add_own(0, m, rows.at[m, rows_of(me), :], mine(before[m]), own_rows)

        to_section(0).wait_recv()
        start_spread(0, 0)
        finish_spread(0, 0)
        second(0)
        to_section(1).wait_recv()
        start_spread(0, 1)
        reduce_core(0)
        finish_spread(0, 1)
        second(1)
        reduce_chip(1, 0)
        start_spread(1, 0)
        reduce_core(1)
        finish_spread(1, 0)
        reduce_chip(1, 1)
        start_spread(1, 1)
        for m in range(micro):
            if m == 1:
                finish_spread(1, 1)
            spread_done(1, m)
            add_own(1, m, own_rows.at[m], mine(selects[m].astype(BF16)), result)
            out_copy(m).start()
        wait_sends()
        for m in range(micro):
            out_copy(m).wait()

    for copy in first:
        copy.wait_send()


def body(tokens_in, norm_gains, w_gate, w_up, w_down, route_ids, route_gates):
    n = lax.axis_size("tensor")
    micro, rpd, width = tokens_in.shape
    chips = n // 2
    cols = width // chips
    tok = n * rpd
    hidden = w_gate.shape[-1]
    picked = route_ids[0] == 0
    chosen = jnp.sum(picked.astype(F32), axis=-1)
    weight = jnp.sum(jnp.where(picked, route_gates[0], 0.0), axis=-1)
    route = jnp.concatenate([chosen, weight, jnp.zeros((8 - 2 * micro, tok), F32)], axis=0)
    dma = pltpu.SemaphoreType.DMA
    out = pl.pallas_call(
        functools.partial(kernel, n, micro),
        out_shape=jax.ShapeDtypeStruct((micro, rpd, width), BF16),
        in_specs=[
            pl.BlockSpec(memory_space=pl.ANY),
            pl.BlockSpec(memory_space=pltpu.VMEM),
            pl.BlockSpec(memory_space=pltpu.VMEM),
            pl.BlockSpec(memory_space=pl.ANY),
            pl.BlockSpec(memory_space=pl.ANY),
            pl.BlockSpec(memory_space=pl.ANY),
        ],
        out_specs=pl.BlockSpec(memory_space=pl.ANY),
        scratch_shapes=[
            pltpu.VMEM((micro, tok, width), BF16),
            pltpu.VMEM((width, hidden), BF16),
            pltpu.VMEM((width, hidden), BF16),
            pltpu.VMEM((hidden, width), BF16),
            pltpu.VMEM((8, tok), F32),
            pltpu.VMEM((micro, CAP, width), F32),
            pltpu.VMEM((micro, chips, CAP, cols), BF16),
            pltpu.VMEM((micro, chips, HALF, cols), BF16),
            pltpu.VMEM((micro, chips, HALF, cols), BF16),
            pltpu.VMEM((micro, chips, HALF, cols), BF16),
            pltpu.VMEM((2, micro, chips, CAP, cols), BF16),
            pltpu.VMEM((micro, rpd, width), BF16),
            pltpu.VMEM((micro, rpd, width), BF16),
            dma((micro,)),
            dma((3,)),
            dma((micro,)),
            dma((2,)),
            dma((micro, chips)),
            dma((micro, n)),
            dma((micro, chips)),
            dma((micro,)),
            dma((micro,)),
            dma((micro, chips)),
            dma((micro, chips)),
            dma((micro,)),
            dma((micro,)),
            dma((2, micro, chips)),
            dma((2, micro, chips)),
            dma((2, micro, chips)),
            dma((2, micro, chips)),
        ],
        compiler_params=pltpu.CompilerParams(
            collective_id=0, has_side_effects=True, vmem_limit_bytes=48 * 1024 * 1024
        ),
        cost_estimate=pl.CostEstimate(flops=2 * 10**9, bytes_accessed=8 * 10**6, transcendentals=10**5),
        name="relay",
    )(tokens_in, norm_gains, route, w_gate[0, 0], w_up[0, 0], w_down[0, 0])
    return out[None]


def solution(mesh):
    return jax.shard_map(
        body,
        mesh=mesh,
        in_specs=(
            P(None, ("dp", "tensor"), None),
            P("section", None),
            P("section", None, None, "tensor"),
            P("section", None, None, "tensor"),
            P("section", None, "tensor", None),
            P("section", None, "dp", None),
            P("section", None, "dp", None),
        ),
        out_specs=P("section", None, ("dp", "tensor"), None),
        check_vma=False,
    )
```

time: 237 us -> 74.8 us (0.32)
  waiting for transfers between devices: 158 us -> 0 us
  Pallas kernels: 0 us -> 67.8 us
  other arithmetic: 29.4 us -> 0.8 us
  matrix products: 15.8 us -> 0 us
  between operations: 13.7 us -> 0.02 us
  local copies, waits for them, and re-layouts: 14.6 us -> 5.61 us
  starting transfers between devices: 3.09 us -> 0 us
    reduce_scatter x3 -> x0, waiting for transfers between devices: 83.7 us -> none  [body(): lax.psum_scatter(partial_value.astype(jnp.bfloat16), 'tensor', scatter_di...]
    pallas_call x0 -> x1, Pallas kernels: none -> 67.8 us  [body(): pl.pallas_call(functools.partial(kernel, n, micro), out_shape=jax.ShapeDt...]
    all_gather x3 -> x0, waiting for transfers between devices: 53.2 us -> none  [body(): whole_rows = lax.all_gather(normed, 'tensor', axis=0, tiled=True)]
    ppermute x2 -> x0, waiting for transfers between devices: 21.1 us -> none  [shifted(): return lax.ppermute(block, axis, route)]
    dot_general x9 -> x0, matrix products: 15.8 us -> none  [the longest x3 8.02 us: expert_partial(): result = jnp.dot(act, down_part[0], preferred_element_type=jnp.float32)]
    convert_element_type x7 -> x0, other arithmetic: 15.5 us -> none  [the longest x3 10.7 us: body(): partial_value.astype(jnp.bfloat16)]
    gather x3 -> x0, local copies, waits for them, and re-layouts: 10.2 us -> none  [expert_partial(): back = jnp.take(result, jnp.clip(slot, 0, CAP - 1), axis=0)]
    another operation x8 -> x0, other arithmetic: 6.06 us -> none  [the longest x2 3.07 us: body(): return jnp.stack(blocks)[None]]
  transfers between devices with their start and end apart: 8 -> 0, of which waited for: 8 -> 0; matrix products, arithmetic and copies ran while one was open for 4% -> 0% of each run, Pallas kernels for 0% -> 0%
where the time goes in v1:
time: 74.8 us; the launch traced here: 74.2 us
  Pallas kernels  67.8 us (91%)
  local copies, waits for them, and re-layouts  5.61 us (8%)
  other arithmetic  0.8 us (1%)
    pallas_call x1, Pallas kernels, body(): pl.pallas_call(functools.partial(kernel, n, micro), out_shape=jax.ShapeDt...  67.8 us
    unnamed x9, local copies, waits for them, and re-layouts  5.54 us

profile of v1, /device:TPU:27, one launch (start us, length us, event | category | flops | bytes accessed | tf_op | source)
XLA Modules:
  0.0 74.2 jit_solution(6369141551333353851)
XLA Ops:
  0.0 0.1 pad.2.clone
  0.1 0.7 convert_reduce_fusion
  0.8 0.1 maximum_maximum_fusion.route_ref
  0.9 0.0 copy-start
  0.9 1.4 %copy-done = bf16[1,1,3072,256]{3,2,1,0:T(8,128)(2,1)S(1)} copy-done((bf16[1,1,3072,256]{3,2,1,0:T(8,128)(2,1)S(1)}, bf16[1,1,3072,256]{3,2,1,0:T(8,128)(2,1)}, u32[]{:S(2)}) %copy-start) | copy-done | bytes 1572888
  2.3 0.0 copy-start.1
  2.3 1.4 %copy-done.1 = bf16[1,1,3072,256]{3,2,1,0:T(8,128)(2,1)S(1)} copy-done((bf16[1,1,3072,256]{3,2,1,0:T(8,128)(2,1)S(1)}, bf16[1,1,3072,256]{3,2,1,0:T(8,128)(2,1)}, u32[]{:S(2)}) %copy-start.1) | copy-done | bytes 1572888
  3.7 0.0 copy-start.2
  3.7 1.1 %copy-done.2 = bf16[2,64,3072]{2,1,0:T(8,128)(2,1)S(1)} copy-done((bf16[2,64,3072]{2,1,0:T(8,128)(2,1)S(1)}, bf16[2,64,3072]{2,1,0:T(8,128)(2,1)}, u32[]{:S(2)}) %copy-start.2) | copy-done | bytes 786456
  4.8 0.0 copy-start.3
  4.8 0.7 copy-done.3
  5.5 67.8 %relay.1 = bf16[2,64,3072]{2,1,0:T(8,128)(2,1)S(1)} custom-call(bf16[2,64,3072]{2,1,0:T(8,128)(2,1)S(1)} %copy-done.2, f32[1,3072]{1,0:T(1,128)S(1)} %copy-done.3, f32[8,256]{1,0:T(8,128)S(1)} %maximum_maximum_fusion.route_ref, bf16[3072,256]{1,0:T(8,128)(2,1)S(1)} %bitcast.5, bf16[3072,256]{1,0:T(8,128)(2,1)S(1)} %bitcast.6, bf16[256,3072]{1,0:T(8,128)(2,1)} %bitcast.7), custom_call_target="tpu_custom_call" | custom-call | flops 2000000000 | bytes 8000000 | tf_op jit(solution)/shard_map/relay/pallas_call | solution.py:314
  73.3 0.9 %copy.9 = bf16[1,2,64,3072]{3,2,1,0:T(8,128)(2,1)} copy(bf16[1,2,64,3072]{3,2,1,0:T(8,128)(2,1)S(1)} %bitcast.4) | data formatting | bytes 1572864
  (1 shorter events, 0.0 us)
Async XLA Ops:
  0.9 1.4 %copy-start = (bf16[1,1,3072,256]{3,2,1,0:T(8,128)(2,1)S(1)}, bf16[1,1,3072,256]{3,2,1,0:T(8,128)(2,1)}, u32[]{:S(2)}) copy-start(bf16[1,1,3072,256]{3,2,1,0:T(8,128)(2,1)} %param.9) | copy-start | bytes 4718596
  2.3 1.4 %copy-start.1 = (bf16[1,1,3072,256]{3,2,1,0:T(8,128)(2,1)S(1)}, bf16[1,1,3072,256]{3,2,1,0:T(8,128)(2,1)}, u32[]{:S(2)}) copy-start(bf16[1,1,3072,256]{3,2,1,0:T(8,128)(2,1)} %param.10) | copy-start | bytes 4718596
  3.7 1.1 %copy-start.2 = (bf16[2,64,3072]{2,1,0:T(8,128)(2,1)S(1)}, bf16[2,64,3072]{2,1,0:T(8,128)(2,1)}, u32[]{:S(2)}) copy-start(bf16[2,64,3072]{2,1,0:T(8,128)(2,1)} %tok_ref.1) | copy-start | bytes 2359300
  4.8 0.7 copy-start.3

commit v2 on v1

--- a/solution.py
+++ b/solution.py
@@ -9,6 +9,9 @@
 
 CAP = 128
 HALF = CAP // 2
+PIECES = 4
+STRIP = HALF // PIECES
+SPLIT = 2
 MESH = pl.DeviceIdType.MESH
 F32 = jnp.float32
 BF16 = jnp.bfloat16
@@ -22,7 +25,7 @@
     n, micro, tok_ref, gain_ref, route_ref, wg_hbm, wu_hbm, wd_hbm, out_ref,
     rows, wg, wu, wd, peer_route, blocks, term, from_mate, chip_sum, from_chip, sums, own_rows, result,
     tok_sem, w_sem, out_sem, route_sems,
-    g_send, g_recv, f_send, a_send, a_recv, b_send, b_recv, c_send, c_recv, d_send, d_recv, e_send, e_recv,
+    g_send, g_recv, y_send, y_recv, x_send, x_recv, fy_send, fy_recv, fx_send, fx_recv, a_send, a_recv, b_send, b_recv, c_send, c_recv, d_send, d_recv, e_send, e_recv,
 ):
     chips = n // 2
     rpd = tok_ref.shape[1]
@@ -70,39 +73,68 @@
     pl.semaphore_signal(barrier, inc=1, device_id={"section": other}, device_id_type=MESH)
     pl.semaphore_wait(barrier, chips + 1)
 
-    def gather(m, owner, target, from_tokens, send):
-        place = rows.at[m, rows_of(owner), :]
-        return remote(tok_ref.at[m] if from_tokens else place, place, send, g_recv.at[m, owner], tensor=target)
-
-    first = []
+    span = width // 2 // SPLIT
 
     def route_copy():
         return remote(route_ref, peer_route, route_sems.at[0], route_sems.at[1], section=other)
 
-    route_copy().start()
-    first.append(route_copy())
+    def lanes_of(section, i):
+        return pl.ds(pl.multiple_of(section * (width // 2) + i * span, 128), span)
+
+    def own_to_mate(m):
+        return remote(tok_ref.at[m], rows.at[m, rows_of(me), :], g_send.at[m], g_recv.at[m], tensor=mate)
+
+    def over_chips(m, step, i):
+        lanes = lanes_of(sec, i)
+        return remote(
+            tok_ref.at[m, :, lanes], rows.at[m, rows_of(me), lanes], y_send.at[m, step, i], y_recv.at[m, step, i],
+            tensor=chip_at(step) * 2 + core,
+        )
+
+    def from_step(step):
+        return chip_at(chips - step) * 2 + core
+
+    def over_sections(m, step, i):
+        place = rows.at[m, rows_of(from_step(step)), lanes_of(sec, i)]
+        return remote(place, place, x_send.at[m, step, i], x_recv.at[m, step, i], section=other)
+
+    def pass_own(m, step, i):
+        place = rows.at[m, rows_of(from_step(step)), lanes_of(sec, i)]
+        return remote(place, place, fy_send.at[m, step, i], fy_recv.at[m, step, i], tensor=mate)
+
+    def pass_other(m, step, i):
+        place = rows.at[m, rows_of(from_step(step)), lanes_of(other, i)]
+        return remote(place, place, fx_send.at[m, step, i], fx_recv.at[m, step, i], tensor=mate)
+
+    hops = [(step, i) for step in range(1, chips) for i in range(SPLIT)]
+    first = []
     for m in range(micro):
-        for step in range(1, chips):
-            copy = gather(m, me, chip_at(step) * 2 + core, True, g_send.at[m, step])
-            copy.start()
-            first.append(copy)
-        copy = gather(m, me, mate, True, g_send.at[m, 0])
-        copy.start()
-        first.append(copy)
+        for step, i in hops:
+            over_chips(m, step, i).start()
+            first.append(over_chips(m, step, i))
+        own_to_mate(m).start()
+        first.append(own_to_mate(m))
+        if m == 0:
+            route_copy().start()
+            first.append(route_copy())
 
     def forward(m):
-        for step in range(1, chips):
-            owner = chip_at(step) * 2 + core
-            copy = gather(m, owner, mate, False, f_send.at[m, step])
-            copy.wait_recv()
-            copy.start()
-            sends.append(copy)
+        for step, i in hops:
+            over_chips(m, step, i).wait_recv()
+            go(over_sections(m, step, i))
+            go(pass_own(m, step, i))
+
+    def forward_other(m):
+        for step, i in hops:
+            over_sections(m, step, i).wait_recv()
+            go(pass_other(m, step, i))
 
     def gathered(m):
         own_copy(m).wait()
-        for step in range(chips):
-            owner = chip_at(step) * 2 + (1 - core)
-            gather(m, owner, mate, False, f_send.at[m, step]).wait_recv()
+        own_to_mate(m).wait_recv()
+        for step, i in hops:
+            pass_own(m, step, i).wait_recv()
+            pass_other(m, step, i).wait_recv()
 
     tri = (
         lax.broadcasted_iota(jnp.int32, (tok, tok), 0) <= lax.broadcasted_iota(jnp.int32, (tok, tok), 1)
@@ -144,29 +176,30 @@
     def to_mate(m):
         return remote(term.at[m, :, mate_half, :], from_mate.at[m], a_send.at[m], a_recv.at[m], tensor=mate)
 
-    def to_chip(m, step):
+    def strip(base, p):
+        return pl.ds(pl.multiple_of(base * HALF + p * STRIP, STRIP), STRIP)
+
+    def to_chip(m, step, p):
         there = chip_at(step)
+        at = pl.ds(p * STRIP, STRIP)
         return remote(
-            chip_sum.at[m, there], from_chip.at[m, step], b_send.at[m, step], b_recv.at[m, step],
+            chip_sum.at[m, there, at, :], from_chip.at[m, step, at, :], b_send.at[m, step, p], b_recv.at[m, step, p],
             tensor=there * 2 + core,
         )
 
-    def piece(layer, m, k, half):
-        return sums.at[layer, m, k, half, :]
-
-    def to_section(m):
-        place = piece(0, m, chip, my_half)
-        return remote(place, place, c_send.at[m], c_recv.at[m], section=other)
-
-    def spread(layer, m, step):
-        place = piece(layer, m, chip, my_half)
+    def to_section(m, p):
+        place = sums.at[0, m, chip, strip(core, p), :]
+        return remote(place, place, c_send.at[m, p], c_recv.at[m, p], section=other)
+
+    def spread(layer, m, step, p):
+        place = sums.at[layer, m, chip, strip(core, p), :]
         return remote(
-            place, place, d_send.at[layer, m, step], d_recv.at[layer, m, step], tensor=chip_at(step) * 2 + core
+            place, place, d_send.at[layer, m, step, p], d_recv.at[layer, m, step, p], tensor=chip_at(step) * 2 + core
         )
 
-    def share(layer, m, step, half):
-        place = piece(layer, m, chip_at(step), half)
-        return remote(place, place, e_send.at[layer, m, step], e_recv.at[layer, m, step], tensor=mate)
+    def share(layer, m, step, p):
+        place = sums.at[layer, m, chip_at(chips - step), strip(core, p), :]
+        return remote(place, place, e_send.at[layer, m, step, p], e_recv.at[layer, m, step, p], tensor=mate)
 
     def go(copy):
         copy.start()
@@ -176,30 +209,42 @@
         to_mate(m).wait_recv()
         for k in range(chips):
             chip_sum[m, k] = (term[m, k, my_half, :].astype(F32) + from_mate[m, k].astype(F32)).astype(BF16)
+        for p in range(PIECES):
+            for step in range(1, chips):
+                go(to_chip(m, step, p))
+
+    def reduce_chip(layer, m):
+        for p in range(PIECES):
+            at = slice(p * STRIP, (p + 1) * STRIP)
+            total = chip_sum[m, chip, at, :].astype(F32)
+            for step in range(1, chips):
+                to_chip(m, step, p).wait_recv()
+                total = total + from_chip[m, step, at, :].astype(F32)
+            sums[layer, m, chip, strip(core, p), :] = total.astype(BF16)
+            if layer == 0:
+                go(to_section(m, p))
+            start_spread(layer, m, p)
+
+    def start_spread(layer, m, p):
         for step in range(1, chips):
-            go(to_chip(m, step))
-
-    def reduce_chip(layer, m):
-        total = chip_sum[m, chip].astype(F32)
-        for step in range(1, chips):
-            to_chip(m, step).wait_recv()
-            total = total + from_chip[m, step].astype(F32)
-        sums[layer, m, chip, my_half, :] = total.astype(BF16)
-
-    def start_spread(layer, m):
-        for step in range(1, chips):
-            go(spread(layer, m, step))
-        go(share(layer, m, 0, my_half))
+            go(spread(layer, m, step, p))
+        go(share(layer, m, 0, p))
+
+    def relay(m):
+        for p in range(PIECES):
+            to_section(m, p).wait_recv()
+            start_spread(0, m, p)
 
     def finish_spread(layer, m):
-        for step in range(1, chips):
-            spread(layer, m, step).wait_recv()
-        for step in range(1, chips):
-            go(share(layer, m, step, my_half))
+        for p in range(PIECES):
+            for step in range(1, chips):
+                spread(layer, m, step, p).wait_recv()
+                go(share(layer, m, step, p))
 
     def spread_done(layer, m):
-        for step in range(chips):
-            share(layer, m, step, mate_half).wait_recv()
+        for p in range(PIECES):
+            for step in range(chips):
+                share(layer, m, step, p).wait_recv()
 
     def out_copy(m):
         return pltpu.make_async_copy(result.at[m], out_ref.at[m], out_sem.at[m])
@@ -218,25 +263,23 @@
     @pl.when(sec == 0)
     def _():
         selects = [selection(route_ref, m) for m in range(micro)]
+        forward(0)
+        forward_other(0)
+        gathered(0)
+        take(0, selects[0].astype(BF16))
         for copy in weight_copies():
             copy.wait()
-        forward(0)
-        gathered(0)
-        take(0, selects[0].astype(BF16))
+        forward(1)
         experts(0, selects[0])
-        forward(1)
+        forward_other(1)
         reduce_core(0)
         gathered(1)
         take(1, selects[1].astype(BF16))
         experts(1, selects[1])
         reduce_chip(0, 0)
-        go(to_section(0))
-        start_spread(0, 0)
         reduce_core(1)
         finish_spread(0, 0)
         reduce_chip(0, 1)
-        go(to_section(1))
-        start_spread(0, 1)
         for m in range(micro):
             if m == 1:
                 finish_spread(0, 1)
@@ -251,40 +294,41 @@
     @pl.when(sec == 1)
     def _():
         selects = [selection(route_ref, m) for m in range(micro)]
+        for m in range(micro):
+            forward(m)
+            forward_other(m)
+        route_copy().wait_recv()
+        before = [selection(peer_route, m).astype(BF16) for m in range(micro)]
+        for m in range(micro):
+            gathered(m)
+            take(m, selects[m].astype(BF16))
         for copy in weight_copies():
             copy.wait()
-        route_copy().wait_recv()
-        before = [selection(peer_route, m).astype(BF16) for m in range(micro)]
-        for m in range(micro):
-            forward(m)
-            gathered(m)
-            take(m, selects[m].astype(BF16))
 
         def second(m):
+            link = dot_nt(selects[m].astype(BF16), before[m]).astype(BF16)
+            finish_spread(0, m)
             spread_done(0, m)
-            link = dot_nt(selects[m].astype(BF16), before[m]).astype(BF16)
             for k in range(chips):
                 at = pl.ds(k * cols, cols)
                 more = jnp.dot(link, sums[0, m, k], preferred_element_type=F32)
                 blocks[m, :, at] = (blocks[m, :, at] + more).astype(BF16).astype(F32)
             experts(m, selects[m])
+
+        def keep(m):
             add_own(0, m, rows.at[m, rows_of(me), :], mine(before[m]), own_rows)
 
-        to_section(0).wait_recv()
-        start_spread(0, 0)
-        finish_spread(0, 0)
+        relay(0)
         second(0)
-        to_section(1).wait_recv()
-        start_spread(0, 1)
         reduce_core(0)
-        finish_spread(0, 1)
+        relay(1)
+        keep(0)
         second(1)
         reduce_chip(1, 0)
-        start_spread(1, 0)
         reduce_core(1)
+        keep(1)
         finish_spread(1, 0)
         reduce_chip(1, 1)
-        start_spread(1, 1)
         for m in range(micro):
             if m == 1:
                 finish_spread(1, 1)
@@ -341,22 +385,19 @@
             dma((3,)),
             dma((micro,)),
             dma((2,)),
-            dma((micro, chips)),
-            dma((micro, n)),
-            dma((micro, chips)),
-            dma((micro,)),
-            dma((micro,)),
-            dma((micro, chips)),
-            dma((micro, chips)),
-            dma((micro,)),
-            dma((micro,)),
-            dma((2, micro, chips)),
-            dma((2, micro, chips)),
-            dma((2, micro, chips)),
-            dma((2, micro, chips)),
+            dma((micro,)),
+            dma((micro,)),
+            *[dma((micro, chips, SPLIT)) for _ in range(8)],
+            dma((micro,)),
+            dma((micro,)),
+            dma((micro, chips, PIECES)),
+            dma((micro, chips, PIECES)),
+            dma((micro, PIECES)),
+            dma((micro, PIECES)),
+            *[dma((2, micro, chips, PIECES)) for _ in range(4)],
         ],
         compiler_params=pltpu.CompilerParams(
-            collective_id=0, has_side_effects=True, vmem_limit_bytes=48 * 1024 * 1024
+            collective_id=0, has_side_effects=True, vmem_limit_bytes=63 * 1024 * 1024
         ),
         cost_estimate=pl.CostEstimate(flops=2 * 10**9, bytes_accessed=8 * 10**6, transcendentals=10**5),
         name="relay",

time: 74.8 us -> 68.9 us (0.921)
  local copies, waits for them, and re-layouts: 5.61 us -> 2.14 us
  Pallas kernels: 67.8 us -> 64.6 us
    unnamed x9 -> x1, local copies, waits for them, and re-layouts: 5.54 us -> 2.06 us
    pallas_call x1, Pallas kernels: 67.8 us -> 64.6 us  [body(): pl.pallas_call(functools.partial(kernel, n, micro), out_shape=jax.ShapeDt...]
where the time goes in v2:
time: 68.9 us; the launch traced here: 68.2 us
  Pallas kernels  64.6 us (94%)
  local copies, waits for them, and re-layouts  2.14 us (3%)
  other arithmetic  1.39 us (2%)
    pallas_call x1, Pallas kernels, body(): pl.pallas_call(functools.partial(kernel, n, micro), out_shape=jax.ShapeDt...  64.6 us
    unnamed x1, local copies, waits for them, and re-layouts  2.06 us

profile of v2, /device:TPU:27, one launch (start us, length us, event | category | flops | bytes accessed | tf_op | source)
XLA Modules:
  0.0 68.2 jit_solution(1084804491514417043)
XLA Ops:
  0.0 0.1 pad.2.clone
  0.1 0.7 %convert_reduce_fusion = (f32[2,256]{1,0:T(2,128)S(1)}, f32[2,256]{1,0:T(2,128)S(1)}) fusion(s32[1,2,256,2]{2,3,1,0:T(2,128)} %param.12, f32[1,2,256,2]{2,3,1,0:T(2,128)} %param.13), kind=kLoop, calls=%fused_computation.2 | loop fusion | flops 4096 | bytes 12288 | tf_op jit(solution)/shard_map/reduce_sum | solution.py:354
  0.8 0.7 maximum_maximum_fusion.route_ref
  1.5 64.6 %relay.1 = bf16[2,64,3072]{2,1,0:T(8,128)(2,1)} custom-call(bf16[2,64,3072]{2,1,0:T(8,128)(2,1)} %tok_ref.1, f32[1,3072]{1,0:T(1,128)} %gain_ref.1, f32[8,256]{1,0:T(8,128)} %maximum_maximum_fusion.route_ref, bf16[3072,256]{1,0:T(8,128)(2,1)} %bitcast.5, bf16[3072,256]{1,0:T(8,128)(2,1)} %bitcast.6, bf16[256,3072]{1,0:T(8,128)(2,1)} %bitcast.7), custom_call_target="tpu_custom_call" | custom-call | flops 2000000000 | bytes 8000000 | tf_op jit(solution)/shard_map/relay/pallas_call | solution.py:358
  66.1 2.1 %copy.9 = bf16[1,2,64,3072]{3,2,1,0:T(8,128)(2,1)} copy(bf16[1,2,64,3072]{3,2,1,0:T(8,128)(2,1)} %bitcast.4) | data formatting | bytes 1572864
  (1 shorter events, 0.0 us)

commit v3 on v2

--- a/solution.py
+++ b/solution.py
@@ -11,7 +11,8 @@
 HALF = CAP // 2
 PIECES = 4
 STRIP = HALF // PIECES
-SPLIT = 2
+EVERY = tuple(range(PIECES))
+SPLIT = 4
 MESH = pl.DeviceIdType.MESH
 F32 = jnp.float32
 BF16 = jnp.bfloat16
@@ -106,7 +107,7 @@
         place = rows.at[m, rows_of(from_step(step)), lanes_of(other, i)]
         return remote(place, place, fx_send.at[m, step, i], fx_recv.at[m, step, i], tensor=mate)
 
-    hops = [(step, i) for step in range(1, chips) for i in range(SPLIT)]
+    hops = [(step, i) for i in range(SPLIT) for step in range(1, chips)]
     first = []
     for m in range(micro):
         for step, i in hops:
@@ -118,16 +119,25 @@
             route_copy().start()
             first.append(route_copy())
 
-    def forward(m):
-        for step, i in hops:
+    def forward(m, i):
+        for step in range(1, chips):
             over_chips(m, step, i).wait_recv()
             go(over_sections(m, step, i))
             go(pass_own(m, step, i))
 
-    def forward_other(m):
-        for step, i in hops:
+    def forward_other(m, i):
+        for step in range(1, chips):
             over_sections(m, step, i).wait_recv()
             go(pass_other(m, step, i))
+
+    def forward_rows():
+        lag = max(1, SPLIT - 1)
+        count = micro * SPLIT
+        for at in range(count):
+            forward(at // SPLIT, at % SPLIT)
+            if at >= lag:
+                forward_other((at - lag) // SPLIT, (at - lag) % SPLIT)
+        return [((at) // SPLIT, at % SPLIT) for at in range(count - lag, count)]
 
     def gathered(m):
         own_copy(m).wait()
@@ -187,9 +197,9 @@
             tensor=there * 2 + core,
         )
 
-    def to_section(m, p):
-        place = sums.at[0, m, chip, strip(core, p), :]
-        return remote(place, place, c_send.at[m, p], c_recv.at[m, p], section=other)
+    def to_section(m, step, p):
+        place = sums.at[0, m, chip_at(chips - step), strip(core, p), :]
+        return remote(place, place, c_send.at[m, step, p], c_recv.at[m, step, p], section=other)
 
     def spread(layer, m, step, p):
         place = sums.at[layer, m, chip, strip(core, p), :]
@@ -214,7 +224,7 @@
                 go(to_chip(m, step, p))
 
     def reduce_chip(layer, m):
-        for p in range(PIECES):
+        for p in EVERY:
             at = slice(p * STRIP, (p + 1) * STRIP)
             total = chip_sum[m, chip, at, :].astype(F32)
             for step in range(1, chips):
@@ -222,7 +232,7 @@
                 total = total + from_chip[m, step, at, :].astype(F32)
             sums[layer, m, chip, strip(core, p), :] = total.astype(BF16)
             if layer == 0:
-                go(to_section(m, p))
+                go(to_section(m, 0, p))
             start_spread(layer, m, p)
 
     def start_spread(layer, m, p):
@@ -230,15 +240,18 @@
             go(spread(layer, m, step, p))
         go(share(layer, m, 0, p))
 
-    def relay(m):
-        for p in range(PIECES):
-            to_section(m, p).wait_recv()
-            start_spread(0, m, p)
+    def relay(m, steps):
+        for step in steps:
+            for p in EVERY:
+                to_section(m, step, p).wait_recv()
+                go(share(0, m, step, p))
 
     def finish_spread(layer, m):
-        for p in range(PIECES):
+        for p in EVERY:
             for step in range(1, chips):
                 spread(layer, m, step, p).wait_recv()
+                if layer == 0:
+                    go(to_section(m, step, p))
                 go(share(layer, m, step, p))
 
     def spread_done(layer, m):
@@ -263,15 +276,14 @@
     @pl.when(sec == 0)
     def _():
         selects = [selection(route_ref, m) for m in range(micro)]
-        forward(0)
-        forward_other(0)
+        left = forward_rows()
         gathered(0)
         take(0, selects[0].astype(BF16))
         for copy in weight_copies():
             copy.wait()
-        forward(1)
         experts(0, selects[0])
-        forward_other(1)
+        for m, i in left:
+            forward_other(m, i)
         reduce_core(0)
         gathered(1)
         take(1, selects[1].astype(BF16))
@@ -294,9 +306,8 @@
     @pl.when(sec == 1)
     def _():
         selects = [selection(route_ref, m) for m in range(micro)]
-        for m in range(micro):
-            forward(m)
-            forward_other(m)
+        for m, i in forward_rows():
+            forward_other(m, i)
         route_copy().wait_recv()
         before = [selection(peer_route, m).astype(BF16) for m in range(micro)]
         for m in range(micro):
@@ -307,7 +318,6 @@
 
         def second(m):
             link = dot_nt(selects[m].astype(BF16), before[m]).astype(BF16)
-            finish_spread(0, m)
             spread_done(0, m)
             for k in range(chips):
                 at = pl.ds(k * cols, cols)
@@ -318,23 +328,25 @@
         def keep(m):
             add_own(0, m, rows.at[m, rows_of(me), :], mine(before[m]), own_rows)
 
-        relay(0)
-        second(0)
-        reduce_core(0)
-        relay(1)
-        keep(0)
-        second(1)
-        reduce_chip(1, 0)
-        reduce_core(1)
-        keep(1)
-        finish_spread(1, 0)
-        reduce_chip(1, 1)
-        for m in range(micro):
-            if m == 1:
-                finish_spread(1, 1)
+        def finish(m):
+            finish_spread(1, m)
             spread_done(1, m)
             add_own(1, m, own_rows.at[m], mine(selects[m].astype(BF16)), result)
             out_copy(m).start()
+
+        relay(0, range(chips))
+        second(0)
+        reduce_core(0)
+        keep(0)
+        relay(1, range(1))
+        reduce_chip(1, 0)
+        relay(1, range(1, chips))
+        second(1)
+        reduce_core(1)
+        keep(1)
+        finish(0)
+        reduce_chip(1, 1)
+        finish(1)
         wait_sends()
         for m in range(micro):
             out_copy(m).wait()
@@ -392,8 +404,8 @@
             dma((micro,)),
             dma((micro, chips, PIECES)),
             dma((micro, chips, PIECES)),
-            dma((micro, PIECES)),
-            dma((micro, PIECES)),
+            dma((micro, chips, PIECES)),
+            dma((micro, chips, PIECES)),
             *[dma((2, micro, chips, PIECES)) for _ in range(4)],
         ],
         compiler_params=pltpu.CompilerParams(

time: 68.9 us -> 65 us (0.943)
  Pallas kernels: 64.6 us -> 61.1 us
    pallas_call x1, Pallas kernels: 64.6 us -> 61.1 us  [body(): pl.pallas_call(functools.partial(kernel, n, micro), out_shape=jax.ShapeDt...]
where the time goes in v3:
time: 65 us; the launch traced here: 64.6 us
  Pallas kernels  61.1 us (94%)
  local copies, waits for them, and re-layouts  2.14 us (3%)
  other arithmetic  1.39 us (2%)
    pallas_call x1, Pallas kernels, body(): pl.pallas_call(functools.partial(kernel, n, micro), out_shape=jax.ShapeDt...  61.1 us
    unnamed x1, local copies, waits for them, and re-layouts  2.06 us

profile of v3, /device:TPU:27, one launch (start us, length us, event | category | flops | bytes accessed | tf_op | source)
XLA Modules:
  0.0 64.6 jit_solution(6142947285195265926)
XLA Ops:
  0.0 0.1 pad.2.clone
  0.1 0.7 %convert_reduce_fusion = (f32[2,256]{1,0:T(2,128)S(1)}, f32[2,256]{1,0:T(2,128)S(1)}) fusion(s32[1,2,256,2]{2,3,1,0:T(2,128)} %param.12, f32[1,2,256,2]{2,3,1,0:T(2,128)} %param.13), kind=kLoop, calls=%fused_computation.2 | loop fusion | flops 4096 | bytes 12288 | tf_op jit(solution)/shard_map/reduce_sum | solution.py:366
  0.8 0.7 %maximum_maximum_fusion.route_ref = f32[8,256]{1,0:T(8,128)} fusion(f32[2,256]{1,0:T(2,128)S(1)} %get-tuple-element.6, f32[2,256]{1,0:T(2,128)S(1)} %get-tuple-element.5, f32[8]{0:T(128)S(1)} %pad.2.clone), kind=kLoop, calls=%fused_computation | loop fusion | flops 4096 | bytes 12320 | tf_op jit(solution)/shard_map/concatenate | solution.py:368
  1.5 61.1 %relay.1 = bf16[2,64,3072]{2,1,0:T(8,128)(2,1)} custom-call(bf16[2,64,3072]{2,1,0:T(8,128)(2,1)} %tok_ref.1, f32[1,3072]{1,0:T(1,128)} %gain_ref.1, f32[8,256]{1,0:T(8,128)} %maximum_maximum_fusion.route_ref, bf16[3072,256]{1,0:T(8,128)(2,1)} %bitcast.5, bf16[3072,256]{1,0:T(8,128)(2,1)} %bitcast.6, bf16[256,3072]{1,0:T(8,128)(2,1)} %bitcast.7), custom_call_target="tpu_custom_call" | custom-call | flops 2000000000 | bytes 8000000 | tf_op jit(solution)/shard_map/relay/pallas_call | solution.py:370
  62.6 2.1 %copy.9 = bf16[1,2,64,3072]{3,2,1,0:T(8,128)(2,1)} copy(bf16[1,2,64,3072]{3,2,1,0:T(8,128)(2,1)} %bitcast.4) | data formatting | bytes 1572864
  (1 shorter events, 0.0 us)

commit v4 on v3

--- a/solution.py
+++ b/solution.py
@@ -292,9 +292,8 @@
         reduce_core(1)
         finish_spread(0, 0)
         reduce_chip(0, 1)
+        finish_spread(0, 1)
         for m in range(micro):
-            if m == 1:
-                finish_spread(0, 1)
             spread_done(0, m)
             add_own(0, m, rows.at[m, rows_of(me), :], mine(selects[m].astype(BF16)), result)
             out_copy(m).start()

time: 65 us -> 65 us (level)
  no operation moved by 1% of the time
where the time goes in v4:
time: 65 us; the launch traced here: 64.6 us
  Pallas kernels  61.1 us (94%)
  local copies, waits for them, and re-layouts  2.14 us (3%)
  other arithmetic  1.39 us (2%)
    pallas_call x1, Pallas kernels, body(): pl.pallas_call(functools.partial(kernel, n, micro), out_shape=jax.ShapeDt...  61.1 us
    unnamed x1, local copies, waits for them, and re-layouts  2.06 us

profile of v4, /device:TPU:27, one launch (start us, length us, event | category | flops | bytes accessed | tf_op | source)
XLA Modules:
  0.0 64.6 jit_solution(10795049758260035222)
XLA Ops:
  0.0 0.1 pad.2.clone
  0.1 0.7 %convert_reduce_fusion = (f32[2,256]{1,0:T(2,128)S(1)}, f32[2,256]{1,0:T(2,128)S(1)}) fusion(s32[1,2,256,2]{2,3,1,0:T(2,128)} %param.12, f32[1,2,256,2]{2,3,1,0:T(2,128)} %param.13), kind=kLoop, calls=%fused_computation.2 | loop fusion | flops 4096 | bytes 12288 | tf_op jit(solution)/shard_map/reduce_sum | solution.py:365
  0.8 0.7 %maximum_maximum_fusion.route_ref = f32[8,256]{1,0:T(8,128)} fusion(f32[2,256]{1,0:T(2,128)S(1)} %get-tuple-element.6, f32[2,256]{1,0:T(2,128)S(1)} %get-tuple-element.5, f32[8]{0:T(128)S(1)} %pad.2.clone), kind=kLoop, calls=%fused_computation | loop fusion | flops 4096 | bytes 12320 | tf_op jit(solution)/shard_map/concatenate | solution.py:367
  1.5 61.1 %relay.1 = bf16[2,64,3072]{2,1,0:T(8,128)(2,1)} custom-call(bf16[2,64,3072]{2,1,0:T(8,128)(2,1)} %tok_ref.1, f32[1,3072]{1,0:T(1,128)} %gain_ref.1, f32[8,256]{1,0:T(8,128)} %maximum_maximum_fusion.route_ref, bf16[3072,256]{1,0:T(8,128)(2,1)} %bitcast.5, bf16[3072,256]{1,0:T(8,128)(2,1)} %bitcast.6, bf16[256,3072]{1,0:T(8,128)(2,1)} %bitcast.7), custom_call_target="tpu_custom_call" | custom-call | flops 2000000000 | bytes 8000000 | tf_op jit(solution)/shard_map/relay/pallas_call | solution.py:369
  62.6 2.1 %copy.9 = bf16[1,2,64,3072]{3,2,1,0:T(8,128)(2,1)} copy(bf16[1,2,64,3072]{3,2,1,0:T(8,128)(2,1)} %bitcast.4) | data formatting | bytes 1572864
  (1 shorter events, 0.0 us)
